TPU v7x, 32 devices: a whole 2x2x4 slice. The times are simulated.
32 devices in a mesh: row: 2 (over x), col: 4 (over y, core), layer: 4 (over z).
Axes of the slice: x: 2, y: 2, z: 4, core: 2. Of those that a mesh axis runs over, the one named last changes fastest.
Arguments:
- a_tiles: bfloat16 [2, 16, 128, 4096], P('row', ('col', 'layer')), may hold values from -0.4375 to 0.4375
- a_rows: int32 [2, 16, 128], P('row', ('col', 'layer')), may hold values from 0 to 31
- a_cols: int32 [2, 16, 128], P('row', ('col', 'layer')), may hold values from 0 to 3
- a_count: int32 [2, 16], P('row', ('col', 'layer')), may hold values from 16 to 128, as said below
- p_tiles: bfloat16 [4, 16, 4, 4096], P('row', ('col', 'layer')), may hold values from -0.375 to 0.375
- p_cols: int32 [4, 16, 4], P('row', ('col', 'layer')), may hold values from -1 to 1
Outputs:
- coarse: float32 [64, 192], replicated
Inputs may be any that keep to these rules, and one draw needn't show every extreme that they name: `a_count`: some device uses all 128 slots and some device only 16 of them.
All inputs are finite; a program needn't handle non-finite values.
Results may differ from a plain program's by a relative error of at most 0.0037.
Values may be sent and summed in bfloat16 or wider, within the bound.
A program may use at most 64 MiB of HBM per device.

v0:
```python
import functools

import jax
import jax.numpy as jnp
from jax import lax
from jax.experimental import pallas as pl
from jax.experimental.pallas import tpu as pltpu
from jax.sharding import PartitionSpec as P

TILE = 64
PB = 1
LANES = 128
CHUNK = 8
MESH = pl.DeviceIdType.MESH


def kernel(
    sizes,
    a_hbm,
    rows_ref,
    cols_ref,
    count_ref,
    p_ref,
    pcols_ref,
    out_ref,
    a_ref,
    wf_ref,
    wb_ref,
    colw_ref,
    roww_ref,
    lhs_ref,
    rhs_ref,
    y_ref,
    y2_ref,
    yrecv_ref,
    ysum_ref,
    part_ref,
    first_ref,
    second_ref,
    third_ref,
    a_sem,
    colw_send,
    colw_recv,
    roww_send,
    roww_recv,
    pair_send,
    pair_recv,
    first_send,
    first_recv,
    second_send,
    second_recv,
    third_send,
    third_recv,
):
    row_devices, col_devices, layer_devices = sizes
    groups = col_devices * layer_devices
    quads = 2 * row_devices
    spots = groups // 2
    local_rows = p_ref.shape[0]
    slots_p = p_ref.shape[2]
    slot_total = a_ref.shape[0]
    pairs = TILE // 2
    block_rows = local_rows * groups
    block_cols = local_rows * row_devices
    my_row = lax.axis_index("row")
    my_col = lax.axis_index("col")
    my_layer = lax.axis_index("layer")
    my_pair = lax.rem(my_col, 2)
    my_quad = my_row * 2 + my_pair
    my_spot = lax.div(my_col, 2) * layer_devices + my_layer

    def place(quad, spot):
        return (
            lax.div(quad, 2),
            lax.div(spot, layer_devices) * 2 + lax.rem(quad, 2),
            lax.rem(spot, layer_devices),
        )

    def around(mine, count, act):
        if count <= 8:
            for k in range(1, count):
                act(lax.rem(mine + k, count))
        else:

            @pl.loop(1, count)
            def _(k):
                act(lax.rem(mine + k, count))

    def send(src, dst, send_sem, recv_sem, device):
        pltpu.make_async_remote_copy(
            src_ref=src,
            dst_ref=dst,
            send_sem=send_sem,
            recv_sem=recv_sem,
            device_id=device,
            device_id_type=MESH,
        ).start()

    def wait_bytes(ref, sem):
        pltpu.make_async_copy(ref, ref, sem).wait()

    barrier = pltpu.get_barrier_semaphore()

    def greet(device):
        pl.semaphore_signal(barrier, inc=1, device_id=device, device_id_type=MESH)

    around(my_spot, spots, lambda peer: greet(place(my_quad, peer)))
    around(my_quad, quads, lambda peer: greet(place(peer, my_spot)))

    a_copy = pltpu.make_async_copy(a_hbm.at[0, 0], a_ref, a_sem)
    a_copy.start()

    slot_ids = lax.broadcasted_iota(jnp.int32, (slots_p, 1), 0)
    for t in range(local_rows):
        tiles = p_ref[t, 0].astype(jnp.float32)
        ids = jnp.full((slots_p, 1), -1, jnp.int32)
        for s in range(slots_p):
            ids = jnp.where(slot_ids == s, pcols_ref[t, 0, s], ids)
        for panel in range(2):
            picked = jnp.sum(jnp.where(ids == panel, tiles, 0.0), axis=0, keepdims=True)
            for j in range(pairs):
                wf_ref[t, j : j + 1, panel * LANES : (panel + 1) * LANES] = picked[
                    :, j * LANES : (j + 1) * LANES
                ]
    own = wf_ref[...].astype(jnp.bfloat16)
    wb_ref[...] = own
    colw_ref[my_row] = own
    roww_ref[my_spot] = own

    pl.semaphore_wait(barrier, spots + quads - 2)
    around(
        my_row,
        row_devices,
        lambda peer: send(
            wb_ref,
            colw_ref.at[my_row],
            colw_send,
            colw_recv,
            place(peer * 2 + my_pair, my_spot),
        ),
    )
    around(
        my_spot,
        spots,
        lambda peer: send(
            wb_ref, roww_ref.at[my_spot], roww_send, roww_recv, place(my_quad, peer)
        ),
    )

    a_copy.wait()
    ids = cols_ref[0] * block_rows + rows_ref[0]
    slot_row = lax.broadcasted_iota(jnp.int32, (1, slot_total), 1)
    ids = jnp.where(slot_row < count_ref[0, 0], ids, -1)
    for c in range(block_cols):
        wanted = c * block_rows + lax.broadcasted_iota(
            jnp.int32, (block_rows, slot_total), 0
        )
        onehot = (ids == wanted).astype(jnp.float32).astype(jnp.bfloat16)
        dense = jnp.dot(onehot, a_ref[...], preferred_element_type=jnp.float32)
        dense = dense.astype(jnp.bfloat16)
        for j in range(pairs):
            lhs_ref[j * block_rows : (j + 1) * block_rows, c * LANES : (c + 1) * LANES] = (
                dense[:, j * LANES : (j + 1) * LANES]
            )

    wait_bytes(colw_ref.at[pl.ds(0, row_devices - 1)], colw_recv)
    out_row = lax.broadcasted_iota(jnp.int32, (LANES, TILE), 0)
    in_row = lax.broadcasted_iota(jnp.int32, (LANES, TILE), 1)
    parity = out_row // TILE
    inner = out_row % TILE
    spread = jnp.where((inner % 2) == parity, 0, pairs) + inner // 2
    spread = (in_row == spread).astype(jnp.float32).astype(jnp.bfloat16)
    lane = lax.broadcasted_iota(jnp.int32, (LANES, 2 * LANES), 1)
    sub = lax.broadcasted_iota(jnp.int32, (LANES, 2 * LANES), 0)
    keep = ((lane // TILE) % 2) == (sub // TILE)
    for c in range(block_cols):
        block = colw_ref[c // local_rows, c % local_rows].astype(jnp.float32)
        swapped = jnp.concatenate(
            [pltpu.roll(block[:, :LANES], TILE, 1), pltpu.roll(block[:, LANES:], TILE, 1)],
            axis=1,
        )
        both = jnp.concatenate([block, swapped], axis=0).astype(jnp.bfloat16)
        made = jnp.dot(spread, both, preferred_element_type=jnp.float32)
        rhs_ref[c * LANES : (c + 1) * LANES, :] = jnp.where(keep, made, 0.0).astype(
            jnp.bfloat16
        )

    y = jnp.dot(lhs_ref[...], rhs_ref[...], preferred_element_type=jnp.float32)
    for h in range(2):
        y_ref[h] = y[:, h * LANES : (h + 1) * LANES]
    def product_rows(pair, spot, t):
        group = (lax.div(spot, layer_devices) * 2 + pair) * layer_devices + lax.rem(
            spot, layer_devices
        )
        return [
            y_ref[h, pl.ds(t * groups + group, pairs, stride=block_rows), :]
            for h in range(2)
        ]

    for spot in range(spots):
        for t in range(local_rows):
            at = (spot * local_rows + t) * pairs
            for h, rows in enumerate(product_rows(1 - my_pair, spot, t)):
                y2_ref[at : at + pairs, h * LANES : (h + 1) * LANES] = rows.astype(
                    jnp.bfloat16
                )
    sibling = place(my_row * 2 + 1 - my_pair, my_spot)
    send(y2_ref, yrecv_ref, pair_send, pair_recv, sibling)
    wait_bytes(yrecv_ref, pair_recv)
    for spot in range(spots):
        for t in range(local_rows):
            at = (spot * local_rows + t) * pairs
            for h, rows in enumerate(product_rows(my_pair, spot, t)):
                spans = (slice(at, at + pairs), slice(h * LANES, (h + 1) * LANES))
                ysum_ref[spans] = (rows + yrecv_ref[spans].astype(jnp.float32)).astype(
                    jnp.bfloat16
                )

    wait_bytes(roww_ref.at[pl.ds(0, spots - 1)], roww_recv)
    window = roww_ref[...].reshape(spots * local_rows * pairs, 2 * LANES)
    m = lax.dot_general(
        window,
        ysum_ref[...],
        (((0,), (0,)), ((), ())),
        preferred_element_type=jnp.float32,
    )

    def fold(i, j):
        top = m[i * LANES : i * LANES + TILE, j * LANES : (j + 1) * LANES]
        low = m[i * LANES + TILE : (i + 1) * LANES, j * LANES : (j + 1) * LANES]
        return top + pltpu.roll(low, TILE, 1)

    left = lax.broadcasted_iota(jnp.int32, (TILE, LANES), 1) < TILE
    upper = jnp.where(left, fold(0, 0), pltpu.roll(fold(0, 1), TILE, 1))
    corner = fold(1, 1)
    lower = jnp.where(
        left[: TILE // 2], corner[: TILE // 2], pltpu.roll(corner[TILE // 2 :], TILE, 1)
    )
    packed = [upper, lower]
    spare = part_ref.shape[0] * part_ref.shape[1] - TILE - TILE // 2
    if spare:
        packed.append(jnp.zeros((spare, LANES), jnp.float32))
    part_ref[...] = jnp.concatenate(packed, axis=0).reshape(part_ref.shape)

    around(
        my_quad,
        quads,
        lambda peer: send(
            part_ref.at[peer],
            first_ref.at[my_quad],
            first_send,
            first_recv,
            place(peer, my_spot),
        ),
    )
    first_ref[my_quad] = part_ref[my_quad]
    wait_bytes(first_ref.at[pl.ds(0, quads - 1)], first_recv)
    second_ref[my_spot] = jnp.sum(first_ref[...], axis=0)
    around(
        my_spot,
        spots,
        lambda peer: send(
            second_ref.at[my_spot],
            second_ref.at[my_spot],
            second_send,
            second_recv,
            place(my_quad, peer),
        ),
    )
    wait_bytes(second_ref.at[pl.ds(0, spots - 1)], second_recv)
    third_ref[my_quad] = jnp.sum(second_ref[...], axis=0)
    around(
        my_quad,
        quads,
        lambda peer: send(
            third_ref.at[my_quad],
            third_ref.at[my_quad],
            third_send,
            third_recv,
            place(peer, my_spot),
        ),
    )
    wait_bytes(third_ref.at[pl.ds(0, quads - 1)], third_recv)

    summed = third_ref[...].reshape(-1, LANES)
    out_ref[:, :LANES] = summed[:TILE]
    corner = summed[TILE : TILE + TILE // 2]
    out_ref[: TILE // 2, LANES:] = corner[:, :TILE]
    out_ref[TILE // 2 :, LANES:] = pltpu.roll(corner, TILE, 1)[:, :TILE]
    wait_bytes(colw_ref.at[pl.ds(0, row_devices - 1)], colw_send)
    wait_bytes(roww_ref.at[pl.ds(0, spots - 1)], roww_send)
    wait_bytes(y2_ref, pair_send)
    wait_bytes(first_ref.at[pl.ds(0, quads - 1)], first_send)
    wait_bytes(second_ref.at[pl.ds(0, spots - 1)], second_send)
    wait_bytes(third_ref.at[pl.ds(0, quads - 1)], third_send)


def per_device(a_tiles, a_rows, a_cols, a_count, p_tiles, p_cols):
    row_devices = lax.axis_size("row")
    col_devices = lax.axis_size("col")
    layer_devices = lax.axis_size("layer")
    groups = col_devices * layer_devices
    spots = groups // 2
    quads = 2 * row_devices
    local_rows = p_tiles.shape[0]
    slot_total = a_tiles.shape[2]
    pairs = TILE // 2
    block_rows = local_rows * groups
    block_cols = local_rows * row_devices
    packed_rows = TILE + TILE // 2
    chunk = pl.cdiv(pl.cdiv(packed_rows, quads), CHUNK) * CHUNK
    half_rows = spots * local_rows * pairs
    sizes = (row_devices, col_devices, layer_devices)
    vmem = pl.BlockSpec(memory_space=pltpu.VMEM)
    smem = pl.BlockSpec(memory_space=pltpu.SMEM)
    wide = 2 * LANES
    return pl.pallas_call(
        functools.partial(kernel, sizes),
        out_shape=jax.ShapeDtypeStruct((PB * TILE, 3 * PB * TILE), jnp.float32),
        in_specs=[pl.BlockSpec(memory_space=pl.ANY), vmem, vmem, smem, vmem, smem],
        out_specs=vmem,
        scratch_shapes=[
            pltpu.VMEM((slot_total, TILE * TILE), jnp.bfloat16),
            pltpu.VMEM((local_rows, pairs, wide), jnp.float32),
            pltpu.VMEM((local_rows, pairs, wide), jnp.bfloat16),
            pltpu.VMEM((row_devices, local_rows, pairs, wide), jnp.bfloat16),
            pltpu.VMEM((spots, local_rows, pairs, wide), jnp.bfloat16),
            pltpu.VMEM((pairs * block_rows, block_cols * LANES), jnp.bfloat16),
            pltpu.VMEM((block_cols * LANES, wide), jnp.bfloat16),
            pltpu.VMEM((2, pairs * block_rows, LANES), jnp.float32),
            pltpu.VMEM((half_rows, wide), jnp.bfloat16),
            pltpu.VMEM((half_rows, wide), jnp.bfloat16),
            pltpu.VMEM((half_rows, wide), jnp.bfloat16),
            pltpu.VMEM((quads, chunk, LANES), jnp.float32),
            pltpu.VMEM((quads, chunk, LANES), jnp.float32),
            pltpu.VMEM((spots, chunk, LANES), jnp.float32),
            pltpu.VMEM((quads, chunk, LANES), jnp.float32),
        ]
        + [pltpu.SemaphoreType.DMA] * 13,
        compiler_params=pltpu.CompilerParams(
            collective_id=0, has_side_effects=True, vmem_limit_bytes=56 << 20
        ),
    )(a_tiles, a_rows, a_cols, a_count, p_tiles, p_cols)


def solution(mesh):
    placed = (
        P("row", ("col", "layer"), None, None),
        P("row", ("col", "layer"), None),
        P("row", ("col", "layer"), None),
        P("row", ("col", "layer")),
        P("row", ("col", "layer"), None, None),
        P("row", ("col", "layer"), None),
    )
    return jax.shard_map(per_device, mesh=mesh, in_specs=placed, out_specs=P(), check_vma=False)
```

profile of v0, /device:TPU:0, one launch (start us, length us, event | category | flops | bytes accessed | tf_op | source)
XLA Modules:
  0.0 27.3 jit_solution(14568913425274359548)
XLA Ops:
  0.7 25.2 %shard_map.64 = f32[64,192]{1,0:T(8,128)} custom-call(bf16[1,1,128,4096]{3,2,1,0:T(8,128)(2,1)} %a_hbm.1, s32[1,1,128]{2,1,0:T(1,128)} %rows_ref.1, s32[1,1,128]{2,1,0:T(1,128)} %cols_ref.1, s32[1,1]{1,0:T(1,128)S(6)} %copy.8.count_ref, bf16[2,1,4,4096]{3,2,1,0:T(4,128)(2,1)} %p_ref.1, s32[2,1,4]{2,1,0:T(1,128)} %pcols_ref.1), custom_call_target="tpu_custom_call" | custom-call | tf_op jit(solution)/shard_map/pallas_call | solution.py:317
  25.8 1.5 %copy.9 = f32[64,192]{1,0:T(8,128)} copy(f32[64,192]{1,0:T(8,128)} %shard_map.64) | data formatting | bytes 98304
where the time goes:
time: 27.5 us; the launch traced here: 27.3 us
  Pallas kernels  25.2 us (92%)
  local copies, waits for them, and re-layouts  1.47 us (5%)
  between operations  0.66 us (2%)
    pallas_call x1, Pallas kernels, per_device(): pl.pallas_call(functools.partial(kernel, sizes), out_shape=jax.ShapeDtype...  25.2 us
    unnamed x1, local copies, waits for them, and re-layouts  1.47 us

commit v1 on v0

--- a/solution.py
+++ b/solution.py
@@ -316,7 +316,7 @@
     wide = 2 * LANES
     return pl.pallas_call(
         functools.partial(kernel, sizes),
-        out_shape=jax.ShapeDtypeStruct((PB * TILE, 3 * PB * TILE), jnp.float32),
+        out_shape=pltpu.VMEM((PB * TILE, 3 * PB * TILE), jnp.float32),
         in_specs=[pl.BlockSpec(memory_space=pl.ANY), vmem, vmem, smem, vmem, smem],
         out_specs=vmem,
         scratch_shapes=[

time: 27.5 us -> 26 us (0.945)
  local copies, waits for them, and re-layouts: 1.47 us -> 0.63 us
  Pallas kernels: 25.2 us -> 24.5 us
    unnamed x1, local copies, waits for them, and re-layouts: 1.47 us -> 0.63 us
    pallas_call x1, Pallas kernels: 25.2 us -> 24.5 us  [per_device(): pl.pallas_call(functools.partial(kernel, sizes), out_shape=pltpu.VMEM((PB...]
where the time goes in v1:
time: 26 us; the launch traced here: 25.8 us
  Pallas kernels  24.5 us (94%)
  between operations  0.66 us (3%)
  local copies, waits for them, and re-layouts  0.63 us (2%)
    pallas_call x1, Pallas kernels, per_device(): pl.pallas_call(functools.partial(kernel, sizes), out_shape=pltpu.VMEM((PB...  24.5 us
    unnamed x1, local copies, waits for them, and re-layouts  0.63 us

profile of v1, /device:TPU:0, one launch (start us, length us, event | category | flops | bytes accessed | tf_op | source)
XLA Modules:
  0.0 25.8 jit_solution(17294912901354565168)
XLA Ops:
  0.7 24.5 %shard_map.64 = f32[64,192]{1,0:T(8,128)S(1)} custom-call(bf16[1,1,128,4096]{3,2,1,0:T(8,128)(2,1)} %a_hbm.1, s32[1,1,128]{2,1,0:T(1,128)} %rows_ref.1, s32[1,1,128]{2,1,0:T(1,128)} %cols_ref.1, s32[1,1]{1,0:T(1,128)S(6)} %copy.9.count_ref, bf16[2,1,4,4096]{3,2,1,0:T(4,128)(2,1)} %p_ref.1, s32[2,1,4]{2,1,0:T(1,128)} %pcols_ref.1), custom_call_target="tpu_custom_call" | custom-call | tf_op jit(solution)/shard_map/pallas_call | solution.py:317
  25.2 0.6 %copy.8 = f32[64,192]{1,0:T(8,128)} copy(f32[64,192]{1,0:T(8,128)S(1)} %shard_map.64) | data formatting | bytes 98304
